TPU v7x, 32 devices: a whole 2x2x4 slice. The times are simulated.
32 devices in a mesh: seq: 8 (over z, y), clip: 4 (over x, core).
Axes of the slice: x: 2, y: 2, z: 4, core: 2. Of those that a mesh axis runs over, the one named last changes fastest.
Arguments:
- tokens: bfloat16 [12288, 1536], P(('clip', 'seq')), parts along dimension 0, may hold values from -16 to 16
- w_qkv: bfloat16 [1536, 2304], P('seq'), may hold values from -0.15625 to 0.15625
- w_out: bfloat16 [768, 1536], P(None, 'seq'), may hold values from -0.21875 to 0.21875
- key_blocks: int32 [192, 4], P(('clip', 'seq')), parts along dimension 0, may hold values from 0 to 47, as said below
- key_levels: int32 [192, 4], P(('clip', 'seq')), parts along dimension 0, may hold values from 1 to 2
Outputs:
- mixed: bfloat16 [12288, 1536], P(('clip', 'seq')), parts along dimension 0
There are 4 independent parts, one for each index of `clip`. A program takes and returns all parts, laid end to end along the dimension named above; an argument that names none is the same for every part. Nothing has to cross between parts.
Inputs may be any that keep to these rules, and one draw needn't show every extreme that they name: `key_blocks`: among the 24 entries of the query blocks of one device (aligned rows of 6), the blocks of any one device (block // 6) are named at most 3 times, and in every draw the blocks of some device exactly 3 times.
All inputs are finite; a program needn't handle non-finite values.
Results may differ from a plain program's by a relative error of at most 0.012.
The roundings to bfloat16 on the way count: a program that leaves them out, or rounds other values in their place, can miss the bound.
Values may be sent and summed in bfloat16 or wider, within the bound.
A program may use at most 128 MiB of HBM per device.

v0:
```python
import math

import jax
import jax.numpy as jnp
from jax import lax
from jax.sharding import PartitionSpec as P

HEADS = 6
HD = 128
BLK = 64
QUART = 16


masked_score = -1e30


def with_halo(block, sides, width):
    for axis, dim in sides:
        count = lax.axis_size(axis)
        forward = [(i, i + 1) for i in range(count - 1)]
        backward = [(target, source) for source, target in forward]
        low = lax.ppermute(
            lax.slice_in_dim(block, block.shape[dim] - width, None, axis=dim), axis, forward
        )
        high = lax.ppermute(lax.slice_in_dim(block, 0, width, axis=dim), axis, backward)
        block = jnp.concatenate([low, block, high], axis=dim)
    return block


def attend(queries, keys_all, score_bias, usable):
    block_count, key_count = (keys_all.shape[0], keys_all.shape[1])
    heads_view = keys_all.reshape(block_count, key_count, 2, HEADS, HD)
    scores = jnp.einsum(
        "bqhd,bkhd->bhqk", queries, heads_view[:, :, 0], preferred_element_type=jnp.float32
    )
    scores = scores * (1.0 / math.sqrt(HD)) + score_bias[:, None, None, :]
    scores = jnp.where(usable[:, None, None, :], scores, masked_score)
    row_top = jnp.max(scores, axis=-1, keepdims=True)
    exponent = jnp.exp(scores - row_top)
    total_mass = jnp.sum(exponent, axis=-1, keepdims=True)
    attn_weights = (exponent / total_mass).astype(jnp.bfloat16)
    attended = jnp.einsum(
        "bhqk,bkhd->bqhd", attn_weights, heads_view[:, :, 1], preferred_element_type=jnp.float32
    )
    return attended.astype(jnp.bfloat16)


def per_device(tokens, w_qkv, w_out, key_blocks, key_levels):
    peer_count = lax.axis_size("seq")
    own_index = lax.axis_index("seq")
    tok_rows = tokens.shape[0]
    local_blocks = tok_rows // BLK
    list_len = key_blocks.shape[1]
    slot_count = (local_blocks * list_len + peer_count - 1) // peer_count
    head_width = HEADS * HD
    projected = jnp.dot(
        tokens, lax.all_gather(w_qkv, "seq", axis=0, tiled=True), preferred_element_type=jnp.float32
    ).astype(jnp.bfloat16)
    queries = projected[:, :head_width]
    key_value = projected[:, head_width:]
    kv_blocks = key_value.reshape(local_blocks, BLK, 2 * head_width)
    widened = kv_blocks.astype(jnp.float32).reshape(
        local_blocks, QUART, BLK // QUART, 2 * head_width
    )
    coarse_own = jnp.mean(widened, axis=2).astype(jnp.bfloat16)
    flat_ids = key_blocks.reshape(-1)
    owner_ids = flat_ids // local_blocks
    local_ids = flat_ids % local_blocks
    peer_ids = jnp.arange(peer_count, dtype=jnp.int32)
    slot_ids = jnp.arange(slot_count, dtype=jnp.int32)
    owner_hot = (owner_ids[:, None] == peer_ids[None, :]).astype(jnp.int32)
    slot_rank = jnp.sum((jnp.cumsum(owner_hot, axis=0) - owner_hot) * owner_hot, axis=1)
    slot_hot = (slot_rank[:, None] == slot_ids[None, :]).astype(jnp.int32)
    wanted = jnp.sum(
        owner_hot[:, :, None] * slot_hot[:, None, :] * local_ids[:, None, None], axis=0
    )
    received = lax.all_to_all(
        coarse_own[lax.all_to_all(wanted, "seq", split_axis=0, concat_axis=0, tiled=True)],
        "seq",
        split_axis=0,
        concat_axis=0,
        tiled=True,
    )
    coarse_rows = received[owner_ids, slot_rank]
    single_rows = jnp.mean(coarse_rows.astype(jnp.float32), axis=1).astype(jnp.bfloat16)
    padded = with_halo(kv_blocks, (("seq", 0),), 1)
    near_rows = jnp.concatenate([padded[:-2], padded[1:-1], padded[2:]], axis=1)
    near_ids = (
        own_index * local_blocks
        + jnp.arange(local_blocks, dtype=jnp.int32)[:, None]
        + jnp.arange(3, dtype=jnp.int32)[None, :]
        - 1
    )
    near_ok = (near_ids >= 0) & (near_ids < local_blocks * peer_count)
    keys_all = jnp.concatenate(
        [
            near_rows,
            coarse_rows.reshape(local_blocks, list_len * QUART, 2 * head_width),
            single_rows.reshape(local_blocks, list_len, 2 * head_width),
        ],
        axis=1,
    )
    usable = jnp.concatenate(
        [
            jnp.repeat(near_ok, BLK, axis=1),
            jnp.repeat(key_levels == 1, QUART, axis=1),
            key_levels == 2,
        ],
        axis=1,
    )
    score_bias = jnp.concatenate(
        [
            jnp.zeros((local_blocks, 3 * BLK), jnp.float32),
            jnp.full((local_blocks, list_len * QUART), math.log(BLK / QUART), jnp.float32),
            jnp.full((local_blocks, list_len), math.log(BLK), jnp.float32),
        ],
        axis=1,
    )
    attended = attend(queries.reshape(local_blocks, BLK, HEADS, HD), keys_all, score_bias, usable)
    attended = attended.reshape(tok_rows, head_width)
    return jnp.dot(
        attended,
        lax.all_gather(w_out, "seq", axis=1, tiled=True),
        preferred_element_type=jnp.float32,
    ).astype(jnp.bfloat16)


def solution(mesh):
    placed = (
        P(("clip", "seq"), None),
        P("seq", None),
        P(None, "seq"),
        P(("clip", "seq"), None),
        P(("clip", "seq"), None),
    )
    return jax.shard_map(
        per_device, mesh=mesh, in_specs=placed, out_specs=P(("clip", "seq"), None), check_vma=False
    )
```

profile of v0, /device:TPU:19, one launch (start us, length us, event | category | flops | bytes accessed | tf_op | source)
XLA Modules:
  0.0 238.8 jit_solution(864172317718418833)
XLA Ops:
  6.5 0.7 all-gather.3.cloned.1.call-update
  7.3 0.7 broadcast_divide_fusion
  8.3 0.7 compare_and_fusion
  9.0 0.1 copy.48
  9.4 0.2 select_reduce_fusion
  9.6 0.1 multiply_reduce_fusion
  9.7 0.7 copy.52
  10.4 5.6 %all-to-all-start = ((s32[8,1,3]{2,1,0:T(1,128)}), s32[8,1,3]{2,1,0:T(1,128)S(1)}, u32[]{:S(2)}, u32[]{:S(2)}) async-start(s32[8,1,3]{2,1,0:T(1,128)} %copy.52), calls=%async_computation | async-start | bytes 8192 | tf_op jit(solution)/shard_map/all_to_all | solution.py:78
  16.0 0.7 all-gather.5.cloned.1.call-update
  16.8 0.7 broadcast_compare_fusion.1
  17.5 1.7 all-to-all-done
  19.5 98.7 %all-gather.3.cloned.1.call-done = bf16[1536,2304]{1,0:T(8,128)(2,1)} async-done(((bf16[192,2304]{1,0:T(8,128)(2,1)}), bf16[1536,2304]{1,0:T(8,128)(2,1)}) %all-gather.3.cloned.1.call-update) | async-done | bytes 7077904 | tf_op jit(solution)/shard_map/all_gather | solution.py:57
  118.1 5.9 %convolution_convert_fusion = bf16[384,2304]{1,0:T(8,128)(2,1)S(1)} fusion(bf16[384,1536]{1,0:T(8,128)(2,1)S(1)} %copy-done, bf16[1536,2304]{1,0:T(8,128)(2,1)} %all-gather.3.cloned.1.call-done), kind=kOutput, calls=%fused_computation.3 | convolution fusion | flops 2718793728 | bytes 10027008 | tf_op jit(solution)/shard_map/dot_general | solution.py:56
  124.0 1.2 copy-done.4
  125.3 1.8 slice_convert_fusion
  127.0 3.4 %reshape.218 = f32[6,16,4,1536]{3,2,1,0:T(4,128)} reshape(f32[384,1536]{1,0:T(8,128)} %get-tuple-element.7) | data formatting | bytes 4718592 | tf_op jit(solution)/shard_map/convert_element_type | solution.py:62
  130.5 3.1 %reduce_sum.47 = f32[6,16,1536]{2,1,0:T(8,128)S(1)} reduce(f32[6,16,4,1536]{3,2,1,0:T(4,128)} %reshape.218, f32[]{:T(128)} %constant.19.clone.1), dimensions={2}, to_apply=%region_0.0 | reduce | flops 442368 | bytes 2949124 | tf_op jit(solution)/shard_map/reduce_sum | solution.py:65
  133.6 1.7 gather_fusion
  135.3 5.4 %all-to-all-start.1 = ((bf16[8,3,16,1536]{3,2,1,0:T(8,128)(2,1)}), bf16[8,3,16,1536]{3,2,1,0:T(8,128)(2,1)}, u32[]{:S(2)}, u32[]{:S(2)}) async-start(bf16[8,3,16,1536]{3,2,1,0:T(8,128)(2,1)} %bitcast.38), calls=%async_computation.1 | async-start | bytes 2359296 | tf_op jit(solution)/shard_map/all_to_all | solution.py:77
  140.8 0.1 copy.55
  140.9 0.6 and.34
  141.5 0.1 copy.62
  141.8 0.1 copy.63
  142.2 1.1 slice_bitcast_fusion.8
  143.2 3.1 %collective-permute-start = (bf16[1,64,1536]{2,1,0:T(8,128)(2,1)S(1)}, bf16[1,64,1536]{2,1,0:T(8,128)(2,1)S(1)}, u32[]{:S(2)}, u32[]{:S(2)}) collective-permute-start(bf16[1,64,1536]{2,1,0:T(8,128)(2,1)S(1)} %get-tuple-element.10), channel_id=1, source_target_pairs={{0,4},{4,8},{8,12},{12,16},{16,20},{20,24},{24,28},{1,5},{5,9},{9,... | collective-permute-start | bytes 589832 | tf_op jit(solution)/shard_map/ppermute | solution.py:22
  146.3 3.1 %collective-permute-start.1 = (bf16[1,64,1536]{2,1,0:T(8,128)(2,1)S(1)}, bf16[1,64,1536]{2,1,0:T(8,128)(2,1)}, u32[]{:S(2)}, u32[]{:S(2)}) collective-permute-start(bf16[1,64,1536]{2,1,0:T(8,128)(2,1)S(1)} %get-tuple-element.9), channel_id=1, source_target_pairs={{4,0},{8,4},{12,8},{16,12},{20,16},{24,20},{28,24},{5,1},{9,5},{13... | collective-permute-start | bytes 589832 | tf_op jit(solution)/shard_map/ppermute | solution.py:25
  149.4 0.7 fusion.22
  150.1 2.2 concatenate.27
  152.3 1.6 reshape.216
  153.9 37.8 %collective-permute-done = bf16[1,64,1536]{2,1,0:T(8,128)(2,1)S(1)} collective-permute-done((bf16[1,64,1536]{2,1,0:T(8,128)(2,1)S(1)}, bf16[1,64,1536]{2,1,0:T(8,128)(2,1)S(1)}, u32[]{:S(2)}, u32[]{:S(2)}) %collective-permute-start) | collective-permute-done | bytes 196640 | tf_op jit(solution)/shard_map/ppermute | solution.py:22
  191.6 0.7 copy-done.6
  192.3 2.2 pad_maximum_fusion
  194.6 2.2 concatenate.26
  196.8 3.9 %concatenate.29 = bf16[6,64,2,6,128]{4,3,2,1,0:T(8,128)(2,1)} reshape(bf16[6,64,1536]{2,1,0:T(8,128)(2,1)} %get-tuple-element.11) | data formatting | bytes 2359296 | tf_op jit(solution)/shard_map/concatenate | solution.py:95
  200.7 2.9 %copy_dynamic-update-slice_fusion.3 = bf16[6,260,2,6,128]{4,1,3,0,2:T(8,128)(2,1)} fusion(bf16[6,64,2,6,128]{4,3,2,1,0:T(8,128)(2,1)} %concatenate.26), kind=kLoop, calls=%fused_computation.25 | loop fusion | bytes 2359296
  203.7 1.4 copy_dynamic-update-slice_fusion.2
  205.0 1.4 copy_dynamic-update-slice_fusion.1
  206.5 1.9 gather_fusion.1
  208.4 2.3 concatenate.31
  210.7 0.4 convert_reduce_fusion
  211.2 2.8 %copy_dynamic-update-slice_fusion = bf16[6,260,2,6,128]{4,1,3,0,2:T(8,128)(2,1)} fusion(bf16[6,260,2,6,128]{4,1,3,0,2:T(8,128)(2,1)} %copy_dynamic-update-slice_fusion.1, bf16[6,64,2,6,128]{4,3,2,1,0:T(8,128)(2,1)} %concatenate.31), kind=kLoop, calls=%fused_computation.22 | loop fusion | bytes 2752512
  214.1 0.7 copy_dynamic-update-slice_fusion.4
  214.7 2.9 %fusion.1 = f32[6,6,64,260]{3,2,1,0:T(8,128)S(1)} fusion(bf16[6,260,2,6,128]{4,1,3,0,2:T(8,128)(2,1)} %copy_dynamic-update-slice_fusion.4, bf16[6,64,6,128]{3,2,1,0:T(8,128)(2,1)S(1)} %copy-done.5), kind=kOutput, calls=%fused_computation.9 | convolution fusion | flops 153354240 | bytes 5419008 | tf_op jit(solution)/shard_map/bqhd,bkhd->bhqk/dot_general | solution.py:33
  217.7 1.9 copy-done.3
  219.6 1.2 fusion.29
  220.8 6.9 %fusion.9 = bf16[6,64,6,128]{3,1,2,0:T(8,128)(2,1)S(1)} fusion(f32[6,6,64]{2,1,0:T(8,128)S(1)} %fusion.29, bf16[6,260,2,6,128]{4,1,3,0,2:T(8,128)(2,1)} %copy_dynamic-update-slice_fusion.4, f32[6,6,64,260]{3,2,1,0:T(8,128)} %copy-done.3, f32[6,260]{1,0:T(8,128)S(1)} %copy-done.7, pred[6,260]{1,0:T(8,128)(4,1)S(1)} %pad_add_fusion), kind=kOutput, calls=%fused_computation.19 | convolution fusion | flops 157245952 | bytes 6578808 | tf_op jit(solution)/shard_map/bhqk,bkhd->bqhd/dot_general | solution.py:42
  227.7 0.4 copy.65
  228.2 3.8 %convolution_convert_fusion.1 = bf16[384,1536]{1,0:T(8,128)(2,1)} fusion(bf16[768,1536]{0,1:T(8,128)(2,1)} %all-gather.5.cloned.1.call-done, bf16[48,8,6,128]{3,2,1,0:T(8,128)(2,1)S(1)} %bitcast.39), kind=kOutput, calls=%fused_computation.7 | convolution fusion | flops 906559488 | bytes 4128768 | tf_op jit(solution)/shard_map/dot_general | solution.py:121
  (46 shorter events, 1.7 us)
Async XLA Ops:
  6.5 111.6 %copy-start = (bf16[384,1536]{1,0:T(8,128)(2,1)S(1)}, bf16[384,1536]{1,0:T(8,128)(2,1)}, u32[]{:S(2)}) copy-start(bf16[384,1536]{1,0:T(8,128)(2,1)} %param.5) | copy-start | bytes 3538948
  6.5 111.6 %all-gather.3.cloned.1.call-start = ((), (), s32[]{:S(2)}) async-start(), calls=%async_computation.2 | async-start | bytes 7962624 | tf_op jit(solution)/shard_map/all_gather | solution.py:57
  10.4 8.8 %all-to-all-start = ((s32[8,1,3]{2,1,0:T(1,128)}), s32[8,1,3]{2,1,0:T(1,128)S(1)}, u32[]{:S(2)}, u32[]{:S(2)}) async-start(s32[8,1,3]{2,1,0:T(1,128)} %copy.52), calls=%async_computation | async-start | bytes 8192 | tf_op jit(solution)/shard_map/all_to_all | solution.py:78
  16.0 212.1 %all-gather.5.cloned.1.call-start = ((), (), s32[]{:S(2)}) async-start(), calls=%async_computation.3 | async-start | bytes 2654208 | tf_op jit(solution)/shard_map/all_gather | solution.py:123
  124.0 1.2 copy-start.4
  135.3 71.2 %all-to-all-start.1 = ((bf16[8,3,16,1536]{3,2,1,0:T(8,128)(2,1)}), bf16[8,3,16,1536]{3,2,1,0:T(8,128)(2,1)}, u32[]{:S(2)}, u32[]{:S(2)}) async-start(bf16[8,3,16,1536]{3,2,1,0:T(8,128)(2,1)} %bitcast.38), calls=%async_computation.1 | async-start | bytes 2359296 | tf_op jit(solution)/shard_map/all_to_all | solution.py:77
  140.7 11.7 %slice-start = ((bf16[384,2304]{1,0:T(8,128)(2,1)}), bf16[384,768]{1,0:T(8,128)(2,1)S(1)}, s32[]{:S(2)}) async-start(bf16[384,2304]{1,0:T(8,128)(2,1)} %copy-done.4), calls=%async_computation.4 | async-start | bytes 1179648 | tf_op jit(solution)/shard_map/slice | solution.py:59
  143.2 48.4 %collective-permute-start = (bf16[1,64,1536]{2,1,0:T(8,128)(2,1)S(1)}, bf16[1,64,1536]{2,1,0:T(8,128)(2,1)S(1)}, u32[]{:S(2)}, u32[]{:S(2)}) collective-permute-start(bf16[1,64,1536]{2,1,0:T(8,128)(2,1)S(1)} %get-tuple-element.10), channel_id=1, source_target_pairs={{0,4},{4,8},{8,12},{12,16},{16,20},{20,24},{24,28},{1,5},{5,9},{9,... | collective-permute-start | bytes 589832 | tf_op jit(solution)/shard_map/ppermute | solution.py:22
  146.3 45.3 %collective-permute-start.1 = (bf16[1,64,1536]{2,1,0:T(8,128)(2,1)S(1)}, bf16[1,64,1536]{2,1,0:T(8,128)(2,1)}, u32[]{:S(2)}, u32[]{:S(2)}) collective-permute-start(bf16[1,64,1536]{2,1,0:T(8,128)(2,1)S(1)} %get-tuple-element.9), channel_id=1, source_target_pairs={{4,0},{8,4},{12,8},{16,12},{20,16},{24,20},{28,24},{5,1},{9,5},{13... | collective-permute-start | bytes 589832 | tf_op jit(solution)/shard_map/ppermute | solution.py:25
  191.6 0.7 copy-start.6
  196.8 6.9 %copy-start.1 = (bf16[6,64,2,6,128]{4,3,2,1,0:T(8,128)(2,1)S(1)}, bf16[6,64,2,6,128]{4,3,2,1,0:T(8,128)(2,1)}, u32[]{:S(2)}) copy-start(bf16[6,64,2,6,128]{4,3,2,1,0:T(8,128)(2,1)} %concatenate.27) | copy-start | bytes 3538948
  200.7 4.3 %copy-start.2 = (bf16[6,64,2,6,128]{4,3,2,1,0:T(8,128)(2,1)S(1)}, bf16[6,64,2,6,128]{4,3,2,1,0:T(8,128)(2,1)}, u32[]{:S(2)}) copy-start(bf16[6,64,2,6,128]{4,3,2,1,0:T(8,128)(2,1)} %concatenate.29) | copy-start | bytes 3538948
  210.7 4.0 %copy-start.5 = (bf16[6,64,6,128]{3,2,1,0:T(8,128)(2,1)S(1)}, bf16[6,64,6,128]{3,2,1,0:T(8,128)(2,1)}, u32[]{:S(2)}) copy-start(bf16[6,64,6,128]{3,2,1,0:T(8,128)(2,1)} %reshape.216) | copy-start | bytes 1769476
  214.7 4.8 %copy-start.7 = (f32[6,260]{1,0:T(8,128)S(1)}, f32[6,260]{1,0:T(8,128)}, u32[]{:S(2)}) copy-start(f32[6,260]{1,0:T(8,128)} %constant.60.clone.1) | copy-start | bytes 18724
  217.7 1.9 copy-start.3
Sparse Core Ops, SparseCore 0:
  9.5 108.5 all-gather.2
  120.3 67.0 all-gather.4
where the time goes:
time: 239 us
  waiting for transfers between devices  140 us (59%)
  local copies, waits for them, and re-layouts  36.8 us (15%)
  matrix products  19.5 us (8%)
  starting transfers between devices  17.1 us (7%)
  between operations  13.5 us (6%)
  other arithmetic  12.2 us (5%)
    all_gather x1, waiting for transfers between devices, per_device(): lax.all_gather(w_qkv, 'seq', axis=0, tiled=True)  98.7 us
    ppermute x1, waiting for transfers between devices, with_halo(): lax.ppermute(lax.slice_in_dim(block, block.shape[dim] - width, None, axis...  37.8 us
    unnamed x20, local copies, waits for them, and re-layouts  12.4 us
    concatenate x5, local copies, waits for them, and re-layouts, per_device(): jnp.concatenate([near_rows, coarse_rows.reshape(local_blocks, list_len *...  11.3 us
    dot_general x1, matrix products, attend(): jnp.einsum('bhqk,bkhd->bqhd', attn_weights, heads_view[:, :, 1], preferre...  6.89 us
    dot_general x1, matrix products, per_device(): jnp.dot(tokens, lax.all_gather(w_qkv, 'seq', axis=0, tiled=True), preferr...  5.9 us
    all_to_all x1, starting transfers between devices, per_device(): lax.all_to_all(wanted, 'seq', split_axis=0, concat_axis=0, tiled=True)  5.61 us
    all_to_all x1, starting transfers between devices, per_device(): lax.all_to_all(coarse_own[lax.all_to_all(wanted, 'seq', split_axis=0, con...  5.36 us
  transfers between devices with their start and end apart: 6, of which 3 were waited for; matrix products, arithmetic and copies ran while one was open for 25% of the time, Pallas kernels for 0%

commit v1 on v0

--- a/solution.py
+++ b/solution.py
@@ -1,8 +1,11 @@
+import functools
 import math
 
 import jax
 import jax.numpy as jnp
 from jax import lax
+from jax.experimental import pallas as pl
+from jax.experimental.pallas import tpu as pltpu
 from jax.sharding import PartitionSpec as P
 
 HEADS = 6
@@ -45,7 +48,7 @@
     return attended.astype(jnp.bfloat16)
 
 
-def per_device(tokens, w_qkv, w_out, key_blocks, key_levels):
+def per_device_general(tokens, w_qkv, w_out, key_blocks, key_levels):
     peer_count = lax.axis_size("seq")
     own_index = lax.axis_index("seq")
     tok_rows = tokens.shape[0]
@@ -125,6 +128,340 @@
     ).astype(jnp.bfloat16)
 
 
+MESH = pl.DeviceIdType.MESH
+LANES = 128
+
+
+def fused_kernel(
+    n, blocks, list_len,
+    blocks_ref, levels_ref, tok_ref, w_ref, wo_ref, out_ref,
+    w_all, wo_all, c_all, rows_all, q_all, kv_all, single_all, att_all,
+    ring_send, ring_recv, core_send, core_recv, x_send, x_recv, relay_send, relay_recv,
+    c_send, c_recv, halo_send, halo_recv,
+):
+    me = lax.axis_index("seq")
+    clip = lax.axis_index("clip")
+    half = n // 2
+    own = blocks * BLK
+    listed = blocks * list_len * QUART
+    near = own + 2 * BLK
+    width = HEADS * HD
+
+    def owner_at(pos):
+        pos = lax.rem(pos + 2 * n, n)
+        return jnp.where(pos < half, 2 * pos, 2 * (n - 1 - pos) + 1)
+
+    pos = jnp.where(lax.rem(me, 2) == 0, me // 2, n - 1 - me // 2)
+    ring = ((owner_at(pos + 1), clip), (owner_at(pos - 1), clip))
+    core_q = clip + 1 - 2 * lax.rem(clip, 2)
+    x_q = lax.rem(clip + 2, 4)
+    core_peer, x_peer = (me, core_q), (me, x_q)
+    after, before = (lax.rem(me + 1, n), clip), (lax.rem(me + n - 1, n), clip)
+
+    barrier = pltpu.get_barrier_semaphore()
+    for peer in (*ring, core_peer, x_peer, after, before):
+        pl.semaphore_signal(barrier, inc=1, device_id=peer, device_id_type=MESH)
+    pl.semaphore_wait(barrier, 6)
+
+    def remote(src, dst, send, recv, peer):
+        return pltpu.make_async_remote_copy(
+            src_ref=src, dst_ref=dst, send_sem=send, recv_sem=recv,
+            device_id=peer, device_id_type=MESH,
+        )
+
+    started = []
+
+    def start(copy):
+        copy.start()
+        started.append(copy)
+
+    shards = ((w_ref, w_all), (wo_ref, wo_all))
+
+    def part(ref, slot, t, way):
+        lanes = ref.shape[-1]
+        if t < half:
+            return ref.at[slot]
+        return ref.at[slot, :, pl.ds(way * (lanes // 2), lanes // 2)]
+
+    def owner_from(t, way):
+        return owner_at(pos - t) if way == 0 else owner_at(pos + t)
+
+    def ring_send_step(kind, t):
+        for way in range(2):
+            source, full = shards[kind]
+            owner = owner_from(t - 1, way)
+            slot = owner * 4 + clip
+            src = part(source, clip, t, way) if t == 1 else part(full, slot, t, way)
+            start(remote(
+                src, part(full, slot, t, way),
+                ring_send.at[kind, t - 1, way], ring_recv.at[kind, t - 1, way], ring[way],
+            ))
+
+    def arrive(kind, t, way):
+        full = shards[kind][1]
+        mine = part(full, owner_from(t, way) * 4 + clip, t, way)
+        remote(
+            mine, mine, ring_send.at[kind, t - 1, way], ring_recv.at[kind, t - 1, way], ring[way]
+        ).wait_recv()
+
+    def share(kind, t):
+        full = shards[kind][1]
+        for way in range(2):
+            mine = part(full, owner_from(t, way) * 4 + clip, t, way)
+            at = (kind, t - 1, way)
+            start(remote(mine, mine, x_send.at[at], x_recv.at[at], x_peer))
+            start(remote(mine, mine, core_send.at[at], core_recv.at[at], core_peer))
+
+    def ring_step(kind, t):
+        for way in range(2):
+            arrive(kind, t, way)
+        if t < half:
+            ring_send_step(kind, t + 1)
+        share(kind, t)
+
+    def relay_step(kind, t):
+        full = shards[kind][1]
+        for way in range(2):
+            at = (kind, t - 1, way)
+            theirs = part(full, owner_from(t, way) * 4 + x_q, t, way)
+            remote(theirs, theirs, x_send.at[at], x_recv.at[at], x_peer).wait_recv()
+            start(remote(theirs, theirs, relay_send.at[at], relay_recv.at[at], core_peer))
+
+    def finish_step(kind, t):
+        full = shards[kind][1]
+        for way in range(2):
+            at = (kind, t - 1, way)
+            owner = owner_from(t, way)
+            one = part(full, owner * 4 + core_q, t, way)
+            remote(one, one, core_send.at[at], core_recv.at[at], core_peer).wait_recv()
+            two = part(full, owner * 4 + lax.rem(core_q + 2, 4), t, way)
+            remote(two, two, relay_send.at[at], relay_recv.at[at], core_peer).wait_recv()
+
+    def c_part(owner, t, way):
+        if t < half:
+            return c_all.at[pl.ds(owner * blocks, blocks)]
+        return c_all.at[pl.ds(owner * blocks + way * (blocks // 2), blocks // 2)]
+
+    def c_send_step(t):
+        for way in range(2):
+            piece = c_part(owner_from(t - 1, way), t, way)
+            start(remote(
+                piece, piece, c_send.at[t - 1, way], c_recv.at[t - 1, way], ring[way]
+            ))
+
+    def c_step(t):
+        for way in range(2):
+            piece = c_part(owner_from(t, way), t, way)
+            remote(
+                piece, piece, c_send.at[t - 1, way], c_recv.at[t - 1, way], ring[way]
+            ).wait_recv()
+        if t < half:
+            c_send_step(t + 1)
+
+    ring_send_step(0, 1)
+    start(remote(
+        tok_ref.at[pl.ds(own - BLK, BLK)], rows_all.at[pl.ds(0, BLK)],
+        halo_send.at[0], halo_recv.at[0], after,
+    ))
+    start(remote(
+        tok_ref.at[pl.ds(0, BLK)], rows_all.at[pl.ds(BLK + own, BLK)],
+        halo_send.at[1], halo_recv.at[1], before,
+    ))
+    coarse_count = blocks * QUART
+    fold = BLK // QUART
+    to_row = lax.broadcasted_iota(jnp.int32, (coarse_count, own), 0)
+    from_row = lax.broadcasted_iota(jnp.int32, (coarse_count, own), 1)
+    mean_of = jnp.where(
+        (from_row >= to_row * fold) & (from_row < (to_row + 1) * fold), 1.0 / fold, 0.0
+    ).astype(jnp.bfloat16)
+    means = jnp.dot(mean_of, tok_ref[...], preferred_element_type=jnp.float32)
+    c_all[pl.ds(me * blocks, blocks)] = means.astype(jnp.bfloat16).reshape(
+        blocks, QUART, tok_ref.shape[1]
+    )
+    c_send_step(1)
+    w_all[pl.ds(me * 4, 4)] = w_ref[...]
+    wo_all[pl.ds(me * 4, 4)] = wo_ref[...]
+    rows_all[pl.ds(BLK, own), :] = tok_ref[...]
+
+    for t in range(1, half + 1):
+        ring_step(0, t)
+        if t > 1:
+            relay_step(0, t - 1)
+        c_step(t)
+    ring_send_step(1, 1)
+    relay_step(0, half)
+    for t in range(1, half + 1):
+        finish_step(0, t)
+    for low, high, side, peer in ((0, BLK, 0, after), (BLK + own, near, 1, before)):
+        piece = rows_all.at[pl.ds(low, BLK)]
+        remote(piece, piece, halo_send.at[side], halo_recv.at[side], peer).wait_recv()
+
+    for b in range(blocks):
+        for i in range(list_len):
+            at = near + (b * list_len + i) * QUART
+            rows_all[pl.ds(at, QUART), :] = c_all[blocks_ref[b, i]]
+
+    depth = w_all.shape[0] * w_all.shape[1]
+    tile = 256
+
+    def q_tile(j, carry):
+        columns = pl.ds(pl.multiple_of(j * tile, tile), tile)
+        q_all[:, columns] = jnp.dot(
+            rows_all[pl.ds(BLK, own), :], w_all[:, :, columns].reshape(depth, tile),
+            preferred_element_type=jnp.float32,
+        ).astype(jnp.bfloat16)
+        return carry
+
+    def kv_tile(j, carry):
+        columns = pl.ds(pl.multiple_of(j * tile, tile), tile)
+        there = pl.ds(pl.multiple_of(width + j * tile, tile), tile)
+        kv_all[:, columns] = jnp.dot(
+            rows_all[...], w_all[:, :, there].reshape(depth, tile),
+            preferred_element_type=jnp.float32,
+        ).astype(jnp.bfloat16)
+        return carry
+
+    lax.fori_loop(0, width // tile, q_tile, 0)
+    ring_step(1, 1)
+    lax.fori_loop(0, width // tile, kv_tile, 0)
+    ring_step(1, 2)
+    relay_step(1, 1)
+    lax.fori_loop(width // tile, 2 * width // tile, kv_tile, 0)
+    for t in range(3, half + 1):
+        ring_step(1, t)
+        relay_step(1, t - 1)
+
+    to_row = lax.broadcasted_iota(jnp.int32, (LANES, listed), 0)
+    from_row = lax.broadcasted_iota(jnp.int32, (LANES, listed), 1)
+    one_of = jnp.where(
+        (from_row >= to_row * QUART) & (from_row < (to_row + 1) * QUART), 1.0 / QUART, 0.0
+    ).astype(jnp.bfloat16)
+    single_all[...] = jnp.dot(
+        one_of, kv_all[pl.ds(near, listed), :], preferred_element_type=jnp.float32
+    ).astype(jnp.bfloat16)
+
+    per = list_len * QUART
+    key_count = 3 * BLK + per + LANES
+    lane = lax.broadcasted_iota(jnp.int32, (1, key_count), 1)
+
+    def attend_block(b, carry):
+        bias = jnp.where(lane < 3 * BLK, 0.0, masked_score)
+        bias = jnp.where((lane < BLK) & (me * blocks + b == 0), masked_score, bias)
+        bias = jnp.where(
+            (lane >= 2 * BLK) & (lane < 3 * BLK) & (me * blocks + b == n * blocks - 1),
+            masked_score, bias,
+        )
+        for i in range(list_len):
+            level = levels_ref[b, i]
+            low = 3 * BLK + i * QUART
+            bias = jnp.where(
+                (lane >= low) & (lane < low + QUART) & (level == 1), math.log(BLK / QUART), bias
+            )
+            bias = jnp.where(
+                (lane == 3 * BLK + per + b * list_len + i) & (level == 2), math.log(BLK), bias
+            )
+        q_rows = pl.ds(pl.multiple_of(b * BLK, BLK), BLK)
+        near_rows = pl.ds(pl.multiple_of(b * BLK, BLK), 3 * BLK)
+        far_rows = pl.ds(pl.multiple_of(near + b * per, per), per)
+        for h in range(HEADS):
+            k_lanes = pl.ds(h * HD, HD)
+            v_lanes = pl.ds(width + h * HD, HD)
+            keys = jnp.concatenate(
+                [kv_all[near_rows, k_lanes], kv_all[far_rows, k_lanes], single_all[:, k_lanes]], 0
+            )
+            values = jnp.concatenate(
+                [kv_all[near_rows, v_lanes], kv_all[far_rows, v_lanes], single_all[:, v_lanes]], 0
+            )
+            scores = lax.dot_general(
+                q_all[q_rows, k_lanes], keys, (((1,), (1,)), ((), ())),
+                preferred_element_type=jnp.float32,
+            )
+            scores = scores * (1.0 / math.sqrt(HD)) + bias
+            exponent = jnp.exp(scores - jnp.max(scores, axis=-1, keepdims=True))
+            total = jnp.sum(exponent, axis=-1, keepdims=True)
+            weights = (exponent / total).astype(jnp.bfloat16)
+            att_all[q_rows, k_lanes] = jnp.dot(
+                weights, values, preferred_element_type=jnp.float32
+            ).astype(jnp.bfloat16)
+        return carry
+
+    lax.fori_loop(0, blocks, attend_block, 0)
+
+    relay_step(1, half)
+    for t in range(1, half + 1):
+        finish_step(1, t)
+
+    out_rows = wo_all.shape[0] * wo_all.shape[1]
+    per_tile = 8
+    out_tile = per_tile * wo_all.shape[1]
+
+    for j in range(out_rows // out_tile):
+        out_ref[:, pl.ds(j * out_tile, out_tile)] = lax.dot_general(
+            att_all[...], wo_all[pl.ds(j * per_tile, per_tile)].reshape(out_tile, width),
+            (((1,), (1,)), ((), ())), preferred_element_type=jnp.float32,
+        ).astype(jnp.bfloat16)
+    for copy in started:
+        copy.wait_send()
+
+
+def per_device_fused(tokens, w_qkv, w_out, key_blocks, key_levels):
+    n = lax.axis_size("seq")
+    own, model = tokens.shape
+    blocks, list_len = key_blocks.shape
+    width = HEADS * HD
+    half = n // 2
+    listed = blocks * list_len * QUART
+    near = own + 2 * BLK
+    w_rows = w_qkv.shape[0] // 4
+    wo_rows = w_out.shape[1] // 4
+    bf16 = jnp.bfloat16
+    pair = lambda: pltpu.SemaphoreType.DMA((2, half, 2))
+    vmem = pl.BlockSpec(memory_space=pltpu.VMEM)
+    smem = pl.BlockSpec(memory_space=pltpu.SMEM)
+    return pl.pallas_call(
+        functools.partial(fused_kernel, n, blocks, list_len),
+        out_shape=jax.ShapeDtypeStruct((own, model), bf16),
+        in_specs=[smem, smem, vmem, vmem, vmem],
+        out_specs=vmem,
+        scratch_shapes=[
+            pltpu.VMEM((n * 4, w_rows, 3 * width), bf16),
+            pltpu.VMEM((n * 4, wo_rows, width), bf16),
+            pltpu.VMEM((n * blocks, QUART, model), bf16),
+            pltpu.VMEM((near + listed, model), bf16),
+            pltpu.VMEM((own, width), bf16),
+            pltpu.VMEM((near + listed, 2 * width), bf16),
+            pltpu.VMEM((LANES, 2 * width), bf16),
+            pltpu.VMEM((own, width), bf16),
+            *[pair() for _ in range(8)],
+            pltpu.SemaphoreType.DMA((half, 2)),
+            pltpu.SemaphoreType.DMA((half, 2)),
+            pltpu.SemaphoreType.DMA((2,)),
+            pltpu.SemaphoreType.DMA((2,)),
+        ],
+        compiler_params=pltpu.CompilerParams(
+            collective_id=0, has_side_effects=True, vmem_limit_bytes=56 * 1024 * 1024
+        ),
+    )(
+        key_blocks, key_levels, tokens,
+        w_qkv.reshape(4, w_rows, 3 * width), w_out.T.reshape(4, wo_rows, width),
+    )
+
+
+def per_device(tokens, w_qkv, w_out, key_blocks, key_levels):
+    blocks, list_len = key_blocks.shape
+    fits = (
+        lax.axis_size("clip") == 4
+        and lax.axis_size("seq") in (4, 6, 8)
+        and w_qkv.shape[0] % 64 == 0
+        and w_out.shape[1] % 64 == 0
+        and blocks % 2 == 0
+        and blocks * list_len <= LANES
+        and (3 * BLK + list_len * QUART) % LANES == 0
+    )
+    form = per_device_fused if fits else per_device_general
+    return form(tokens, w_qkv, w_out, key_blocks, key_levels)
+
+
 def solution(mesh):
     placed = (
         P(("clip", "seq"), None),

time: 239 us -> 96.6 us (0.40)
  the two profiles are of different devices: /device:TPU:19 before, /device:TPU:0 now
where the time goes in v1:
time: 96.6 us; the launch traced here: 96 us
  Pallas kernels  90.9 us (94%)
  local copies, waits for them, and re-layouts  5.06 us (5%)
    pallas_call x1, Pallas kernels, per_device_fused(): pl.pallas_call(functools.partial(fused_kernel, n, blocks, list_len), out_...  90.9 us
    unnamed x3, local copies, waits for them, and re-layouts  5.06 us

profile of v1, /device:TPU:0, one launch (start us, length us, event | category | flops | bytes accessed | tf_op | source)
XLA Modules:
  0.0 96.0 jit_solution(14879493697775907656)
XLA Ops:
  0.0 1.4 %copy.6.blocks_ref = s32[6,4]{1,0:T(8,128)} copy(s32[6,4]{0,1:T(4,128)} %param.8) | data formatting | bytes 192 | tf_op args[3]
  1.4 1.4 %copy.7.levels_ref = s32[6,4]{1,0:T(8,128)} copy(s32[6,4]{0,1:T(4,128)} %param.9) | data formatting | bytes 192 | tf_op args[4]
  2.7 90.9 %shard_map.55 = bf16[384,1536]{1,0:T(8,128)(2,1)} custom-call(s32[6,4]{1,0:T(8,128)} %copy.6.blocks_ref, s32[6,4]{1,0:T(8,128)} %copy.7.levels_ref, bf16[384,1536]{1,0:T(8,128)(2,1)} %tok_ref.1, bf16[4,48,2304]{2,1,0:T(8,128)(2,1)} %bitcast.4, bf16[4,48,768]{2,1,0:T(8,128)(2,1)} %bitcast.5), custom_call_target="tpu_custom_call" | custom-call | tf_op jit(solution)/shard_map/pallas_call | solution.py:421
  93.6 2.4 %copy.9 = bf16[384,1536]{1,0:T(8,128)(2,1)} copy(bf16[384,1536]{1,0:T(8,128)(2,1)} %shard_map.55) | data formatting | bytes 2359296

commit v2 on v1

--- a/solution.py
+++ b/solution.py
@@ -135,7 +135,7 @@
 def fused_kernel(
     n, blocks, list_len,
     blocks_ref, levels_ref, tok_ref, w_ref, wo_ref, out_ref,
-    w_all, wo_all, c_all, rows_all, q_all, kv_all, single_all, att_all,
+    w_all, wo_all, c_all, rows_all, q_all, kv_all, pick_all, far_all, att_all,
     ring_send, ring_recv, core_send, core_recv, x_send, x_recv, relay_send, relay_recv,
     c_send, c_recv, halo_send, halo_recv,
 ):
@@ -259,14 +259,6 @@
             c_send_step(t + 1)
 
     ring_send_step(0, 1)
-    start(remote(
-        tok_ref.at[pl.ds(own - BLK, BLK)], rows_all.at[pl.ds(0, BLK)],
-        halo_send.at[0], halo_recv.at[0], after,
-    ))
-    start(remote(
-        tok_ref.at[pl.ds(0, BLK)], rows_all.at[pl.ds(BLK + own, BLK)],
-        halo_send.at[1], halo_recv.at[1], before,
-    ))
     coarse_count = blocks * QUART
     fold = BLK // QUART
     to_row = lax.broadcasted_iota(jnp.int32, (coarse_count, own), 0)
@@ -278,28 +270,47 @@
     c_all[pl.ds(me * blocks, blocks)] = means.astype(jnp.bfloat16).reshape(
         blocks, QUART, tok_ref.shape[1]
     )
+    ring_step(0, 1)
     c_send_step(1)
+    start(remote(
+        tok_ref.at[pl.ds(own - BLK, BLK)], rows_all.at[pl.ds(0, BLK)],
+        halo_send.at[0], halo_recv.at[0], after,
+    ))
+    start(remote(
+        tok_ref.at[pl.ds(0, BLK)], rows_all.at[pl.ds(BLK + own, BLK)],
+        halo_send.at[1], halo_recv.at[1], before,
+    ))
     w_all[pl.ds(me * 4, 4)] = w_ref[...]
     wo_all[pl.ds(me * 4, 4)] = wo_ref[...]
     rows_all[pl.ds(BLK, own), :] = tok_ref[...]
 
-    for t in range(1, half + 1):
+    slab_row = lax.broadcasted_iota(jnp.int32, (QUART, listed), 0)
+    slab_from = lax.broadcasted_iota(jnp.int32, (QUART, listed), 1)
+    for b in range(blocks):
+        for i in range(list_len):
+            at = (b * list_len + i) * QUART
+            level = levels_ref[i, b]
+            inside = (slab_from >= at) & (slab_from < at + QUART)
+            same = jnp.where(slab_from == slab_row + at, 1.0, 0.0)
+            mean = jnp.where(inside, 1.0 / QUART, 0.0)
+            pick_all[pl.ds(at, QUART), :] = jnp.where(
+                (slab_row == 0) & (level == 2), mean, same
+            ).astype(jnp.bfloat16)
+
+    for t in range(2, half + 1):
         ring_step(0, t)
-        if t > 1:
-            relay_step(0, t - 1)
-        c_step(t)
+        relay_step(0, t - 1)
+        if t < half:
+            c_step(t - 1)
+    for t in range(1, half):
+        finish_step(0, t)
+    relay_step(0, half)
+    c_step(half - 1)
     ring_send_step(1, 1)
-    relay_step(0, half)
-    for t in range(1, half + 1):
-        finish_step(0, t)
+    finish_step(0, half)
     for low, high, side, peer in ((0, BLK, 0, after), (BLK + own, near, 1, before)):
         piece = rows_all.at[pl.ds(low, BLK)]
         remote(piece, piece, halo_send.at[side], halo_recv.at[side], peer).wait_recv()
-
-    for b in range(blocks):
-        for i in range(list_len):
-            at = near + (b * list_len + i) * QUART
-            rows_all[pl.ds(at, QUART), :] = c_all[blocks_ref[b, i]]
 
     depth = w_all.shape[0] * w_all.shape[1]
     tile = 256
@@ -312,39 +323,38 @@
         ).astype(jnp.bfloat16)
         return carry
 
-    def kv_tile(j, carry):
+    def kv_tile(low, count, j, carry):
         columns = pl.ds(pl.multiple_of(j * tile, tile), tile)
         there = pl.ds(pl.multiple_of(width + j * tile, tile), tile)
-        kv_all[:, columns] = jnp.dot(
-            rows_all[...], w_all[:, :, there].reshape(depth, tile),
+        kv_all[pl.ds(low, count), columns] = jnp.dot(
+            rows_all[pl.ds(low, count), :], w_all[:, :, there].reshape(depth, tile),
             preferred_element_type=jnp.float32,
         ).astype(jnp.bfloat16)
         return carry
 
-    lax.fori_loop(0, width // tile, q_tile, 0)
+    tiles = width // tile
+    lax.fori_loop(0, tiles, q_tile, 0)
+    lax.fori_loop(0, 2 * tiles, functools.partial(kv_tile, 0, near), 0)
     ring_step(1, 1)
-    lax.fori_loop(0, width // tile, kv_tile, 0)
+    c_step(half)
+
+    for b in range(blocks):
+        for i in range(list_len):
+            at = near + (b * list_len + i) * QUART
+            rows_all[pl.ds(at, QUART), :] = c_all[blocks_ref[i, b]]
+    lax.fori_loop(0, 2 * tiles, functools.partial(kv_tile, near, listed), 0)
+    far_all[...] = jnp.dot(
+        pick_all[...], kv_all[pl.ds(near, listed), :], preferred_element_type=jnp.float32
+    ).astype(jnp.bfloat16)
     ring_step(1, 2)
     relay_step(1, 1)
-    lax.fori_loop(width // tile, 2 * width // tile, kv_tile, 0)
-    for t in range(3, half + 1):
-        ring_step(1, t)
-        relay_step(1, t - 1)
-
-    to_row = lax.broadcasted_iota(jnp.int32, (LANES, listed), 0)
-    from_row = lax.broadcasted_iota(jnp.int32, (LANES, listed), 1)
-    one_of = jnp.where(
-        (from_row >= to_row * QUART) & (from_row < (to_row + 1) * QUART), 1.0 / QUART, 0.0
-    ).astype(jnp.bfloat16)
-    single_all[...] = jnp.dot(
-        one_of, kv_all[pl.ds(near, listed), :], preferred_element_type=jnp.float32
-    ).astype(jnp.bfloat16)
 
     per = list_len * QUART
-    key_count = 3 * BLK + per + LANES
+    key_count = 3 * BLK + per
     lane = lax.broadcasted_iota(jnp.int32, (1, key_count), 1)
-
-    def attend_block(b, carry):
+    log2e = math.log2(math.e)
+
+    def attend_block(b):
         bias = jnp.where(lane < 3 * BLK, 0.0, masked_score)
         bias = jnp.where((lane < BLK) & (me * blocks + b == 0), masked_score, bias)
         bias = jnp.where(
@@ -352,50 +362,47 @@
             masked_score, bias,
         )
         for i in range(list_len):
-            level = levels_ref[b, i]
+            level = levels_ref[i, b]
             low = 3 * BLK + i * QUART
             bias = jnp.where(
-                (lane >= low) & (lane < low + QUART) & (level == 1), math.log(BLK / QUART), bias
+                (lane >= low) & (lane < low + QUART) & (level == 1),
+                math.log2(BLK / QUART), bias,
             )
-            bias = jnp.where(
-                (lane == 3 * BLK + per + b * list_len + i) & (level == 2), math.log(BLK), bias
-            )
-        q_rows = pl.ds(pl.multiple_of(b * BLK, BLK), BLK)
-        near_rows = pl.ds(pl.multiple_of(b * BLK, BLK), 3 * BLK)
-        far_rows = pl.ds(pl.multiple_of(near + b * per, per), per)
+            bias = jnp.where((lane == low) & (level == 2), math.log2(BLK), bias)
+        q_rows = pl.ds(b * BLK, BLK)
+        near_rows = pl.ds(b * BLK, 3 * BLK)
+        far_rows = pl.ds(b * per, per)
         for h in range(HEADS):
             k_lanes = pl.ds(h * HD, HD)
             v_lanes = pl.ds(width + h * HD, HD)
-            keys = jnp.concatenate(
-                [kv_all[near_rows, k_lanes], kv_all[far_rows, k_lanes], single_all[:, k_lanes]], 0
-            )
-            values = jnp.concatenate(
-                [kv_all[near_rows, v_lanes], kv_all[far_rows, v_lanes], single_all[:, v_lanes]], 0
-            )
+            keys = jnp.concatenate([kv_all[near_rows, k_lanes], far_all[far_rows, k_lanes]], 0)
+            values = jnp.concatenate([kv_all[near_rows, v_lanes], far_all[far_rows, v_lanes]], 0)
             scores = lax.dot_general(
                 q_all[q_rows, k_lanes], keys, (((1,), (1,)), ((), ())),
                 preferred_element_type=jnp.float32,
             )
-            scores = scores * (1.0 / math.sqrt(HD)) + bias
-            exponent = jnp.exp(scores - jnp.max(scores, axis=-1, keepdims=True))
+            scores = scores * (log2e / math.sqrt(HD)) + bias
+            exponent = jnp.exp2(scores - jnp.max(scores, axis=-1, keepdims=True))
             total = jnp.sum(exponent, axis=-1, keepdims=True)
-            weights = (exponent / total).astype(jnp.bfloat16)
+            weights = (exponent * (1.0 / total)).astype(jnp.bfloat16)
             att_all[q_rows, k_lanes] = jnp.dot(
                 weights, values, preferred_element_type=jnp.float32
             ).astype(jnp.bfloat16)
-        return carry
-
-    lax.fori_loop(0, blocks, attend_block, 0)
-
-    relay_step(1, half)
+
+    for b in range(blocks):
+        attend_block(b)
+        t = 3 + b
+        if t <= half:
+            ring_step(1, t)
+            relay_step(1, t - 1)
+        elif t == half + 1:
+            relay_step(1, half)
     for t in range(1, half + 1):
         finish_step(1, t)
 
-    out_rows = wo_all.shape[0] * wo_all.shape[1]
     per_tile = 8
     out_tile = per_tile * wo_all.shape[1]
-
-    for j in range(out_rows // out_tile):
+    for j in range(wo_all.shape[0] // per_tile):
         out_ref[:, pl.ds(j * out_tile, out_tile)] = lax.dot_general(
             att_all[...], wo_all[pl.ds(j * per_tile, per_tile)].reshape(out_tile, width),
             (((1,), (1,)), ((), ())), preferred_element_type=jnp.float32,
@@ -430,7 +437,8 @@
             pltpu.VMEM((near + listed, model), bf16),
             pltpu.VMEM((own, width), bf16),
             pltpu.VMEM((near + listed, 2 * width), bf16),
-            pltpu.VMEM((LANES, 2 * width), bf16),
+            pltpu.VMEM((listed, listed), bf16),
+            pltpu.VMEM((listed, 2 * width), bf16),
             pltpu.VMEM((own, width), bf16),
             *[pair() for _ in range(8)],
             pltpu.SemaphoreType.DMA((half, 2)),
@@ -442,7 +450,7 @@
             collective_id=0, has_side_effects=True, vmem_limit_bytes=56 * 1024 * 1024
         ),
     )(
-        key_blocks, key_levels, tokens,
+        key_blocks.T, key_levels.T, tokens,
         w_qkv.reshape(4, w_rows, 3 * width), w_out.T.reshape(4, wo_rows, width),
     )
 
@@ -455,7 +463,7 @@
         and w_qkv.shape[0] % 64 == 0
         and w_out.shape[1] % 64 == 0
         and blocks % 2 == 0
-        and blocks * list_len <= LANES
+        and blocks >= 4
         and (3 * BLK + list_len * QUART) % LANES == 0
     )
     form = per_device_fused if fits else per_device_general

time: 96.6 us -> 87.2 us (0.903)
  Pallas kernels: 90.9 us -> 84.7 us
  local copies, waits for them, and re-layouts: 5.06 us -> 2.36 us
    pallas_call x1, Pallas kernels: 90.9 us -> 84.7 us  [per_device_fused(): pl.pallas_call(functools.partial(fused_kernel, n, blocks, list_len), out_...]
    unnamed x3 -> x1, local copies, waits for them, and re-layouts: 5.06 us -> 2.36 us
where the time goes in v2:
time: 87.2 us; the launch traced here: 87.1 us
  Pallas kernels  84.7 us (97%)
  local copies, waits for them, and re-layouts  2.36 us (3%)
    pallas_call x1, Pallas kernels, per_device_fused(): pl.pallas_call(functools.partial(fused_kernel, n, blocks, list_len), out_...  84.7 us
    unnamed x1, local copies, waits for them, and re-layouts  2.36 us

profile of v2, /device:TPU:0, one launch (start us, length us, event | category | flops | bytes accessed | tf_op | source)
XLA Modules:
  0.0 87.1 jit_solution(17712931343252377978)
XLA Ops:
  0.0 84.7 %shard_map.55 = bf16[384,1536]{1,0:T(8,128)(2,1)} custom-call(s32[4,6]{1,0:T(4,128)} %bitcast.8, s32[4,6]{1,0:T(4,128)} %bitcast.9, bf16[384,1536]{1,0:T(8,128)(2,1)} %tok_ref.1, bf16[4,48,2304]{2,1,0:T(8,128)(2,1)} %bitcast.6, bf16[4,48,768]{2,1,0:T(8,128)(2,1)} %bitcast.7), custom_call_target="tpu_custom_call" | custom-call | tf_op jit(solution)/shard_map/pallas_call | solution.py:428
  84.7 2.4 %copy.7 = bf16[384,1536]{1,0:T(8,128)(2,1)} copy(bf16[384,1536]{1,0:T(8,128)(2,1)} %shard_map.55) | data formatting | bytes 2359296

commit v3 on v2

--- a/solution.py
+++ b/solution.py
@@ -161,7 +161,6 @@
     barrier = pltpu.get_barrier_semaphore()
     for peer in (*ring, core_peer, x_peer, after, before):
         pl.semaphore_signal(barrier, inc=1, device_id=peer, device_id_type=MESH)
-    pl.semaphore_wait(barrier, 6)
 
     def remote(src, dst, send, recv, peer):
         return pltpu.make_async_remote_copy(
@@ -258,7 +257,6 @@
         if t < half:
             c_send_step(t + 1)
 
-    ring_send_step(0, 1)
     coarse_count = blocks * QUART
     fold = BLK // QUART
     to_row = lax.broadcasted_iota(jnp.int32, (coarse_count, own), 0)
@@ -270,16 +268,6 @@
     c_all[pl.ds(me * blocks, blocks)] = means.astype(jnp.bfloat16).reshape(
         blocks, QUART, tok_ref.shape[1]
     )
-    ring_step(0, 1)
-    c_send_step(1)
-    start(remote(
-        tok_ref.at[pl.ds(own - BLK, BLK)], rows_all.at[pl.ds(0, BLK)],
-        halo_send.at[0], halo_recv.at[0], after,
-    ))
-    start(remote(
-        tok_ref.at[pl.ds(0, BLK)], rows_all.at[pl.ds(BLK + own, BLK)],
-        halo_send.at[1], halo_recv.at[1], before,
-    ))
     w_all[pl.ds(me * 4, 4)] = w_ref[...]
     wo_all[pl.ds(me * 4, 4)] = wo_ref[...]
     rows_all[pl.ds(BLK, own), :] = tok_ref[...]
@@ -297,20 +285,49 @@
                 (slab_row == 0) & (level == 2), mean, same
             ).astype(jnp.bfloat16)
 
+    first, last = me == 0, me == n - 1
+
+    @pl.when(first)
+    def _():
+        rows_all[pl.ds(0, BLK), :] = jnp.zeros((BLK, rows_all.shape[1]), jnp.bfloat16)
+
+    @pl.when(last)
+    def _():
+        rows_all[pl.ds(BLK + own, BLK), :] = jnp.zeros((BLK, rows_all.shape[1]), jnp.bfloat16)
+
+    pl.semaphore_wait(barrier, 6)
+
+    ring_send_step(0, 1)
+    ring_step(0, 1)
+    c_send_step(1)
+    up = remote(
+        tok_ref.at[pl.ds(own - BLK, BLK)], rows_all.at[pl.ds(0, BLK)],
+        halo_send.at[0], halo_recv.at[0], after,
+    )
+    down = remote(
+        tok_ref.at[pl.ds(0, BLK)], rows_all.at[pl.ds(BLK + own, BLK)],
+        halo_send.at[1], halo_recv.at[1], before,
+    )
+    pl.when(me < n - 1)(up.start)
+    pl.when(me > 0)(down.start)
     for t in range(2, half + 1):
         ring_step(0, t)
         relay_step(0, t - 1)
+        if t == 2:
+            ring_send_step(1, 1)
+        else:
+            ring_step(1, t - 2)
+            if t > 3:
+                relay_step(1, t - 3)
         if t < half:
             c_step(t - 1)
     for t in range(1, half):
         finish_step(0, t)
     relay_step(0, half)
     c_step(half - 1)
-    ring_send_step(1, 1)
     finish_step(0, half)
-    for low, high, side, peer in ((0, BLK, 0, after), (BLK + own, near, 1, before)):
-        piece = rows_all.at[pl.ds(low, BLK)]
-        remote(piece, piece, halo_send.at[side], halo_recv.at[side], peer).wait_recv()
+    pl.when(me > 0)(up.wait_recv)
+    pl.when(me < n - 1)(down.wait_recv)
 
     depth = w_all.shape[0] * w_all.shape[1]
     tile = 256
@@ -335,7 +352,8 @@
     tiles = width // tile
     lax.fori_loop(0, tiles, q_tile, 0)
     lax.fori_loop(0, 2 * tiles, functools.partial(kv_tile, 0, near), 0)
-    ring_step(1, 1)
+    ring_step(1, half - 1)
+    relay_step(1, half - 2)
     c_step(half)
 
     for b in range(blocks):
@@ -346,8 +364,8 @@
     far_all[...] = jnp.dot(
         pick_all[...], kv_all[pl.ds(near, listed), :], preferred_element_type=jnp.float32
     ).astype(jnp.bfloat16)
-    ring_step(1, 2)
-    relay_step(1, 1)
+    ring_step(1, half)
+    relay_step(1, half - 1)
 
     per = list_len * QUART
     key_count = 3 * BLK + per
@@ -391,11 +409,7 @@
 
     for b in range(blocks):
         attend_block(b)
-        t = 3 + b
-        if t <= half:
-            ring_step(1, t)
-            relay_step(1, t - 1)
-        elif t == half + 1:
+        if b == 2:
             relay_step(1, half)
     for t in range(1, half + 1):
         finish_step(1, t)
@@ -407,6 +421,8 @@
             att_all[...], wo_all[pl.ds(j * per_tile, per_tile)].reshape(out_tile, width),
             (((1,), (1,)), ((), ())), preferred_element_type=jnp.float32,
         ).astype(jnp.bfloat16)
+    pl.when(me < n - 1)(up.wait_send)
+    pl.when(me > 0)(down.wait_send)
     for copy in started:
         copy.wait_send()
 

time: 87.2 us -> 84.4 us (0.968)
  Pallas kernels: 84.7 us -> 81.5 us
    pallas_call x1, Pallas kernels: 84.7 us -> 81.5 us  [per_device_fused(): pl.pallas_call(functools.partial(fused_kernel, n, blocks, list_len), out_...]
where the time goes in v3:
time: 84.4 us; the launch traced here: 83.9 us
  Pallas kernels  81.5 us (97%)
  local copies, waits for them, and re-layouts  2.36 us (3%)
    pallas_call x1, Pallas kernels, per_device_fused(): pl.pallas_call(functools.partial(fused_kernel, n, blocks, list_len), out_...  81.5 us
    unnamed x1, local copies, waits for them, and re-layouts  2.36 us

profile of v3, /device:TPU:0, one launch (start us, length us, event | category | flops | bytes accessed | tf_op | source)
XLA Modules:
  0.0 83.9 jit_solution(8190462425581374682)
XLA Ops:
  0.0 81.5 %shard_map.55 = bf16[384,1536]{1,0:T(8,128)(2,1)} custom-call(s32[4,6]{1,0:T(4,128)} %bitcast.8, s32[4,6]{1,0:T(4,128)} %bitcast.9, bf16[384,1536]{1,0:T(8,128)(2,1)} %tok_ref.1, bf16[4,48,2304]{2,1,0:T(8,128)(2,1)} %bitcast.6, bf16[4,48,768]{2,1,0:T(8,128)(2,1)} %bitcast.7), custom_call_target="tpu_custom_call" | custom-call | tf_op jit(solution)/shard_map/pallas_call | solution.py:444
  81.5 2.4 %copy.7 = bf16[384,1536]{1,0:T(8,128)(2,1)} copy(bf16[384,1536]{1,0:T(8,128)(2,1)} %shard_map.55) | data formatting | bytes 2359296

commit v4 on v3

--- a/solution.py
+++ b/solution.py
@@ -185,8 +185,8 @@
     def owner_from(t, way):
         return owner_at(pos - t) if way == 0 else owner_at(pos + t)
 
-    def ring_send_step(kind, t):
-        for way in range(2):
+    def ring_send_step(kind, t, ways=(0, 1)):
+        for way in ways:
             source, full = shards[kind]
             owner = owner_from(t - 1, way)
             slot = owner * 4 + clip
@@ -203,9 +203,9 @@
             mine, mine, ring_send.at[kind, t - 1, way], ring_recv.at[kind, t - 1, way], ring[way]
         ).wait_recv()
 
-    def share(kind, t):
+    def share(kind, t, ways=(0, 1)):
         full = shards[kind][1]
-        for way in range(2):
+        for way in ways:
             mine = part(full, owner_from(t, way) * 4 + clip, t, way)
             at = (kind, t - 1, way)
             start(remote(mine, mine, x_send.at[at], x_recv.at[at], x_peer))
@@ -214,9 +214,9 @@
     def ring_step(kind, t):
         for way in range(2):
             arrive(kind, t, way)
-        if t < half:
-            ring_send_step(kind, t + 1)
-        share(kind, t)
+            if t < half:
+                ring_send_step(kind, t + 1, (way,))
+            share(kind, t, (way,))
 
     def relay_step(kind, t):
         full = shards[kind][1]
@@ -241,8 +241,8 @@
             return c_all.at[pl.ds(owner * blocks, blocks)]
         return c_all.at[pl.ds(owner * blocks + way * (blocks // 2), blocks // 2)]
 
-    def c_send_step(t):
-        for way in range(2):
+    def c_send_step(t, ways=(0, 1)):
+        for way in ways:
             piece = c_part(owner_from(t - 1, way), t, way)
             start(remote(
                 piece, piece, c_send.at[t - 1, way], c_recv.at[t - 1, way], ring[way]
@@ -254,8 +254,8 @@
             remote(
                 piece, piece, c_send.at[t - 1, way], c_recv.at[t - 1, way], ring[way]
             ).wait_recv()
-        if t < half:
-            c_send_step(t + 1)
+            if t < half:
+                c_send_step(t + 1, (way,))
 
     coarse_count = blocks * QUART
     fold = BLK // QUART
@@ -390,22 +390,33 @@
         q_rows = pl.ds(b * BLK, BLK)
         near_rows = pl.ds(b * BLK, 3 * BLK)
         far_rows = pl.ds(b * per, per)
-        for h in range(HEADS):
-            k_lanes = pl.ds(h * HD, HD)
-            v_lanes = pl.ds(width + h * HD, HD)
-            keys = jnp.concatenate([kv_all[near_rows, k_lanes], far_all[far_rows, k_lanes]], 0)
-            values = jnp.concatenate([kv_all[near_rows, v_lanes], far_all[far_rows, v_lanes]], 0)
-            scores = lax.dot_general(
-                q_all[q_rows, k_lanes], keys, (((1,), (1,)), ((), ())),
-                preferred_element_type=jnp.float32,
-            )
-            scores = scores * (log2e / math.sqrt(HD)) + bias
-            exponent = jnp.exp2(scores - jnp.max(scores, axis=-1, keepdims=True))
-            total = jnp.sum(exponent, axis=-1, keepdims=True)
-            weights = (exponent * (1.0 / total)).astype(jnp.bfloat16)
-            att_all[q_rows, k_lanes] = jnp.dot(
-                weights, values, preferred_element_type=jnp.float32
-            ).astype(jnp.bfloat16)
+        for low in range(0, HEADS, 6):
+            heads = range(low, low + 6)
+            scores = []
+            for h in heads:
+                k_lanes = pl.ds(h * HD, HD)
+                keys = jnp.concatenate(
+                    [kv_all[near_rows, k_lanes], far_all[far_rows, k_lanes]], 0
+                )
+                scores.append(lax.dot_general(
+                    q_all[q_rows, k_lanes], keys, (((1,), (1,)), ((), ())),
+                    preferred_element_type=jnp.float32,
+                ))
+            scores = [s * (log2e / math.sqrt(HD)) + bias for s in scores]
+            tops = [jnp.max(s, axis=-1, keepdims=True) for s in scores]
+            exponents = [jnp.exp2(s - top) for s, top in zip(scores, tops)]
+            totals = [jnp.sum(e, axis=-1, keepdims=True) for e in exponents]
+            weights = [
+                (e * (1.0 / total)).astype(jnp.bfloat16) for e, total in zip(exponents, totals)
+            ]
+            for h, weight in zip(heads, weights):
+                v_lanes = pl.ds(width + h * HD, HD)
+                values = jnp.concatenate(
+                    [kv_all[near_rows, v_lanes], far_all[far_rows, v_lanes]], 0
+                )
+                att_all[q_rows, pl.ds(h * HD, HD)] = jnp.dot(
+                    weight, values, preferred_element_type=jnp.float32
+                ).astype(jnp.bfloat16)
 
     for b in range(blocks):
         attend_block(b)

time: 84.4 us -> 76.9 us (0.911)
  Pallas kernels: 81.5 us -> 74.3 us
    pallas_call x1, Pallas kernels: 81.5 us -> 74.3 us  [per_device_fused(): pl.pallas_call(functools.partial(fused_kernel, n, blocks, list_len), out_...]
where the time goes in v4:
time: 76.9 us; the launch traced here: 76.7 us
  Pallas kernels  74.3 us (97%)
  local copies, waits for them, and re-layouts  2.36 us (3%)
    pallas_call x1, Pallas kernels, per_device_fused(): pl.pallas_call(functools.partial(fused_kernel, n, blocks, list_len), out_...  74.3 us
    unnamed x1, local copies, waits for them, and re-layouts  2.36 us

profile of v4, /device:TPU:0, one launch (start us, length us, event | category | flops | bytes accessed | tf_op | source)
XLA Modules:
  0.0 76.7 jit_solution(16704490783681329787)
XLA Ops:
  0.0 74.3 %shard_map.55 = bf16[384,1536]{1,0:T(8,128)(2,1)} custom-call(s32[4,6]{1,0:T(4,128)} %bitcast.8, s32[4,6]{1,0:T(4,128)} %bitcast.9, bf16[384,1536]{1,0:T(8,128)(2,1)} %tok_ref.1, bf16[4,48,2304]{2,1,0:T(8,128)(2,1)} %bitcast.6, bf16[4,48,768]{2,1,0:T(8,128)(2,1)} %bitcast.7), custom_call_target="tpu_custom_call" | custom-call | tf_op jit(solution)/shard_map/pallas_call | solution.py:455
  74.3 2.4 %copy.7 = bf16[384,1536]{1,0:T(8,128)(2,1)} copy(bf16[384,1536]{1,0:T(8,128)(2,1)} %shard_map.55) | data formatting | bytes 2359296

commit v5 on v4

--- a/solution.py
+++ b/solution.py
@@ -350,8 +350,8 @@
         return carry
 
     tiles = width // tile
-    lax.fori_loop(0, tiles, q_tile, 0)
-    lax.fori_loop(0, 2 * tiles, functools.partial(kv_tile, 0, near), 0)
+    lax.fori_loop(0, tiles, q_tile, 0, unroll=True)
+    lax.fori_loop(0, 2 * tiles, functools.partial(kv_tile, 0, near), 0, unroll=True)
     ring_step(1, half - 1)
     relay_step(1, half - 2)
     c_step(half)
@@ -360,7 +360,7 @@
         for i in range(list_len):
             at = near + (b * list_len + i) * QUART
             rows_all[pl.ds(at, QUART), :] = c_all[blocks_ref[i, b]]
-    lax.fori_loop(0, 2 * tiles, functools.partial(kv_tile, near, listed), 0)
+    lax.fori_loop(0, 2 * tiles, functools.partial(kv_tile, near, listed), 0, unroll=True)
     far_all[...] = jnp.dot(
         pick_all[...], kv_all[pl.ds(near, listed), :], preferred_element_type=jnp.float32
     ).astype(jnp.bfloat16)
@@ -409,19 +409,26 @@
             weights = [
                 (e * (1.0 / total)).astype(jnp.bfloat16) for e, total in zip(exponents, totals)
             ]
-            for h, weight in zip(heads, weights):
-                v_lanes = pl.ds(width + h * HD, HD)
-                values = jnp.concatenate(
-                    [kv_all[near_rows, v_lanes], far_all[far_rows, v_lanes]], 0
-                )
-                att_all[q_rows, pl.ds(h * HD, HD)] = jnp.dot(
-                    weight, values, preferred_element_type=jnp.float32
-                ).astype(jnp.bfloat16)
-
+            def combine():
+                for h, weight in zip(heads, weights):
+                    v_lanes = pl.ds(width + h * HD, HD)
+                    values = jnp.concatenate(
+                        [kv_all[near_rows, v_lanes], far_all[far_rows, v_lanes]], 0
+                    )
+                    att_all[q_rows, pl.ds(h * HD, HD)] = jnp.dot(
+                        weight, values, preferred_element_type=jnp.float32
+                    ).astype(jnp.bfloat16)
+            return combine
+
+    combine = None
     for b in range(blocks):
-        attend_block(b)
+        ahead = attend_block(b)
+        if combine is not None:
+            combine()
+        combine = ahead
         if b == 2:
             relay_step(1, half)
+    combine()
     for t in range(1, half + 1):
         finish_step(1, t)
 

time: 76.9 us -> 75.4 us (0.980)
  Pallas kernels: 74.3 us -> 72.9 us
    pallas_call x1, Pallas kernels: 74.3 us -> 72.9 us  [per_device_fused(): pl.pallas_call(functools.partial(fused_kernel, n, blocks, list_len), out_...]
where the time goes in v5:
time: 75.4 us; the launch traced here: 75.3 us
  Pallas kernels  72.9 us (97%)
  local copies, waits for them, and re-layouts  2.36 us (3%)
    pallas_call x1, Pallas kernels, per_device_fused(): pl.pallas_call(functools.partial(fused_kernel, n, blocks, list_len), out_...  72.9 us
    unnamed x1, local copies, waits for them, and re-layouts  2.36 us

profile of v5, /device:TPU:0, one launch (start us, length us, event | category | flops | bytes accessed | tf_op | source)
XLA Modules:
  0.0 75.3 jit_solution(3780156219215855818)
XLA Ops:
  0.0 72.9 %shard_map.55 = bf16[384,1536]{1,0:T(8,128)(2,1)} custom-call(s32[4,6]{1,0:T(4,128)} %bitcast.8, s32[4,6]{1,0:T(4,128)} %bitcast.9, bf16[384,1536]{1,0:T(8,128)(2,1)} %tok_ref.1, bf16[4,48,2304]{2,1,0:T(8,128)(2,1)} %bitcast.6, bf16[4,48,768]{2,1,0:T(8,128)(2,1)} %bitcast.7), custom_call_target="tpu_custom_call" | custom-call | tf_op jit(solution)/shard_map/pallas_call | solution.py:462
  72.9 2.4 %copy.7 = bf16[384,1536]{1,0:T(8,128)(2,1)} copy(bf16[384,1536]{1,0:T(8,128)(2,1)} %shard_map.55) | data formatting | bytes 2359296
